TPU v7x, 128 devices: a whole 4x4x4 slice. The times are simulated.
128 devices in a mesh: grp: 16 (over z, y_lo, core), tp: 8 (over x, y_hi).
Axes of the slice: x: 4, y: 4 (y_hi: 2, y_lo: 2; y = y_hi * 2 + y_lo), z: 4, core: 2. Of those that a mesh axis runs over, the one named last changes fastest.
Arguments:
- hidden: bfloat16 [512, 16384], P(('grp', 'tp')), may hold values from -130 to 130
- gain: float32 [16384], replicated, may hold values from 0.5 to 1.5
- head: bfloat16 [16384, 65536], P(None, ('grp', 'tp')), may hold values from -3 to 3
Outputs:
- log_probs: float32 [512, 65536], P(('grp', 'tp'))
All inputs are finite; a program needn't handle non-finite values.
Results may differ from a plain program's by a relative error of at most 0.00055.
Values may be sent and summed in bfloat16 or wider, within the bound.
A program may use at most 128 MiB of HBM per device.

v0:
```python
import jax
import jax.numpy as jnp
from jax import lax
from jax.sharding import PartitionSpec as P


def in_order(pieces, dim):
    pieces = jnp.moveaxis(pieces, 0, dim)
    dims = pieces.shape
    return pieces.reshape(*dims[:dim], dims[dim] * dims[dim + 1], *dims[dim + 2 :])


def sent_to_all(array, axis):
    count = lax.axis_size(axis)
    return lax.all_to_all(
        jnp.broadcast_to(array[None], (count, *array.shape)), axis, 0, 0, tiled=True
    )


def collect(array, axis, dim):
    return in_order(sent_to_all(array, axis), dim)


def on_device(hidden, gain, head):
    values = hidden.astype(jnp.float32)
    mean_square = jnp.mean(values * values, axis=-1, keepdims=True)
    normed = (values * lax.rsqrt(mean_square + 1e-05) * gain).astype(jnp.bfloat16)
    group_block = collect(normed, "tp", 0)
    logits = jnp.dot(
        lax.all_gather(group_block, "grp", axis=0, tiled=True),
        head,
        preferred_element_type=jnp.float32,
    )
    owned = lax.all_to_all(logits, ("grp", "tp"), split_axis=0, concat_axis=1, tiled=True)
    top = jnp.max(owned, axis=-1, keepdims=True)
    total = jnp.sum(jnp.exp(owned - top), axis=-1, keepdims=True)
    return owned - top - jnp.log(total)


def solution(mesh):
    return jax.shard_map(
        on_device,
        mesh=mesh,
        in_specs=(P(("grp", "tp"), None), P(), P(None, ("grp", "tp"))),
        out_specs=P(("grp", "tp"), None),
        check_vma=False,
    )
```

profile of v0, /device:TPU:1, one launch (start us, length us, event | category | flops | bytes accessed | tf_op | source)
XLA Modules:
  0.0 179.9 jit_solution(17725672794546746063)
XLA Ops:
  6.5 0.0 all-gather.2.cloned.1.call-start
  6.5 1.2 fusion.2
  7.7 1.0 fusion.4
  8.7 0.3 broadcast_in_dim.2
  9.0 22.5 %all_to_all.24 = bf16[8,4,16384]{2,1,0:T(4,128)(2,1)S(1)} all-to-all(bf16[8,4,16384]{2,1,0:T(4,128)(2,1)S(1)} %broadcast_in_dim.2), channel_id=1, replica_groups=mesh['grp'=16,'tp'=8] {'tp'}, dimensions={0} | all-to-all | bytes 2097152 | tf_op jit(solution)/shard_map/all_to_all | solution.py:15
  31.6 1.1 reshape.25
  32.6 0.0 all-gather.2.cloned.1.call-update
  32.7 92.8 %all-gather.2.cloned.1.call-done = bf16[512,16384]{1,0:T(8,128)(2,1)} async-done(((bf16[32,16384]{1,0:T(8,128)(2,1)}), bf16[512,16384]{1,0:T(8,128)(2,1)}) %all-gather.2.cloned.1.call-update) | async-done | bytes 16777232 | tf_op jit(solution)/shard_map/all_gather | solution.py:30
  125.4 16.4 %fusion.5 = f32[512,512]{1,0:T(8,128)S(1)} fusion(bf16[512,16384]{1,0:T(8,128)(2,1)} %all-gather.2.cloned.1.call-done, bf16[16384,512]{1,0:T(8,128)(2,1)} %param.5), kind=kOutput, calls=%fused_computation.10 | convolution fusion | flops 8589934592 | bytes 34603008 | tf_op jit(solution)/shard_map/dot_general | solution.py:29
  141.9 0.3 all_to_all.18
  142.2 28.3 %all_to_all.25 = f32[128,4,512]{2,1,0:T(4,128)S(1)} all-to-all(f32[128,4,512]{2,1,0:T(4,128)S(1)} %all_to_all.18), channel_id=1, replica_groups=mesh['grp'=16,'tp'=8] {'grp','tp'}, dimensions={0} | all-to-all | bytes 2097152 | tf_op jit(solution)/shard_map/all_to_all | solution.py:34
  170.4 0.7 reduce_max.9
  171.1 0.7 fusion.1
  171.8 1.2 subtract_subtract_fusion
  (2 shorter events, 0.0 us)
Async XLA Ops:
  6.5 118.9 %all-gather.2.cloned.1.call-start = ((), (), s32[]{:S(2)}) async-start(), calls=%async_computation.2 | async-start | bytes 17825792 | tf_op jit(solution)/shard_map/all_gather | solution.py:30
Sparse Core Ops, SparseCore 0:
  32.8 92.5 all-gather.1
where the time goes:
time: 180 us
  waiting for transfers between devices  92.8 us (52%)
  blocking collectives  50.8 us (28%)
  matrix products  16.4 us (9%)
  between operations  13.4 us (7%)
  other arithmetic  4.83 us (3%)
    all_gather x1, waiting for transfers between devices, on_device(): lax.all_gather(group_block, 'grp', axis=0, tiled=True)  92.8 us
    all_to_all x1, blocking collectives, on_device(): lax.all_to_all(logits, ('grp', 'tp'), split_axis=0, concat_axis=1, tiled=...  28.3 us
    all_to_all x1, blocking collectives, sent_to_all(): lax.all_to_all(jnp.broadcast_to(array[None], (count, *array.shape)), axis...  22.5 us
    dot_general x1, matrix products, on_device(): jnp.dot(lax.all_gather(group_block, 'grp', axis=0, tiled=True), head, pre...  16.4 us
  transfers between devices with their start and end apart: 1, of which 1 were waited for; matrix products, arithmetic and copies ran while one was open for 0% of the time, Pallas kernels for 0%

commit v1 on v0

--- a/solution.py
+++ b/solution.py
@@ -27,7 +27,9 @@
     normed = (values * lax.rsqrt(mean_square + 1e-05) * gain).astype(jnp.bfloat16)
     group_block = collect(normed, "tp", 0)
     logits = jnp.dot(
-        lax.all_gather(group_block, "grp", axis=0, tiled=True),
+        jnp.concatenate(
+            lax.all_to_all(jnp.stack([group_block] * lax.axis_size("grp")), "grp", 0, 0), axis=0
+        ),
         head,
         preferred_element_type=jnp.float32,
     )

time: 180 us -> 300 us (1.67)
  blocking collectives: 50.8 us -> 239 us
  waiting for transfers between devices: 92.8 us -> 0 us
  local copies, waits for them, and re-layouts: 1.68 us -> 27.8 us
  between operations: 13.4 us -> 0.05 us
  matrix products: 16.4 us -> 27.4 us
    all_to_all x0 -> x1, blocking collectives: none -> 192 us  [on_device(): lax.all_to_all(jnp.stack([group_block] * lax.axis_size('grp')), 'grp', 0, 0)]
    all_gather x1 -> x0, waiting for transfers between devices: 92.8 us -> none  [on_device(): lax.all_gather(group_block, 'grp', axis=0, tiled=True)]
    dot_general x0 -> x2, local copies, waits for them, and re-layouts: none -> 25.5 us  [on_device(): jnp.dot(jnp.concatenate(lax.all_to_all(jnp.stack([group_block] * lax.axis...]
    dot_general x1, matrix products: 16.4 us -> 27.4 us  [on_device(): jnp.dot(jnp.concatenate(lax.all_to_all(jnp.stack([group_block] * lax.axis...]
    all_to_all x1, blocking collectives: 28.3 us -> 24.7 us  [on_device(): lax.all_to_all(logits, ('grp', 'tp'), split_axis=0, concat_axis=1, tiled=...]
  transfers between devices with their start and end apart: 1 -> 0, of which waited for: 1 -> 0; matrix products, arithmetic and copies ran while one was open for 0% -> 0% of each run, Pallas kernels for 0% -> 0%
where the time goes in v1:
time: 300 us; the launch traced here: 299 us
  blocking collectives  239 us (80%)
  local copies, waits for them, and re-layouts  27.8 us (9%)
  matrix products  27.4 us (9%)
  other arithmetic  4.83 us (2%)
    all_to_all x1, blocking collectives, on_device(): lax.all_to_all(jnp.stack([group_block] * lax.axis_size('grp')), 'grp', 0, 0)  192 us
    dot_general x1, matrix products, on_device(): jnp.dot(jnp.concatenate(lax.all_to_all(jnp.stack([group_block] * lax.axis...  27.4 us
    dot_general x2, local copies, waits for them, and re-layouts, on_device(): jnp.dot(jnp.concatenate(lax.all_to_all(jnp.stack([group_block] * lax.axis...  25.5 us
    all_to_all x1, blocking collectives, on_device(): lax.all_to_all(logits, ('grp', 'tp'), split_axis=0, concat_axis=1, tiled=...  24.7 us
    all_to_all x1, blocking collectives, sent_to_all(): lax.all_to_all(jnp.broadcast_to(array[None], (count, *array.shape)), axis...  22.5 us

profile of v1, /device:TPU:1, one launch (start us, length us, event | category | flops | bytes accessed | tf_op | source)
XLA Modules:
  0.0 299.1 jit_solution(6077821142668294026)
XLA Ops:
  0.0 1.2 fusion.5
  1.2 1.0 fusion.7
  2.2 0.3 broadcast_in_dim.2
  2.5 22.5 %all_to_all.26 = bf16[8,4,16384]{2,1,0:T(4,128)(2,1)S(1)} all-to-all(bf16[8,4,16384]{2,1,0:T(4,128)(2,1)S(1)} %broadcast_in_dim.2), channel_id=1, replica_groups=mesh['grp'=16,'tp'=8] {'tp'}, dimensions={0} | all-to-all | bytes 2097152 | tf_op jit(solution)/shard_map/all_to_all | solution.py:15
  25.0 0.3 stack_reshape.2
  25.3 1.7 stack.3
  27.0 191.8 %all_to_all.27 = bf16[16,32,16384]{2,1,0:T(8,128)(2,1)} all-to-all(bf16[16,32,16384]{2,1,0:T(8,128)(2,1)S(1)} %stack.3), channel_id=1, replica_groups=mesh['grp'=16,'tp'=8] {'grp'}, dimensions={0} | all-to-all | bytes 33554432 | tf_op jit(solution)/shard_map/all_to_all | solution.py:31
  218.9 24.8 %dot_general.5 = bf16[128,4,16384]{2,1,0:T(4,128)(2,1)} reshape(bf16[16,32,16384]{2,1,0:T(8,128)(2,1)} %all_to_all.27) | data formatting | bytes 33554432 | tf_op jit(solution)/shard_map/dot_general | solution.py:29
  243.7 27.4 %fusion = f32[128,4,512]{2,0,1:T(8,128)S(1)} fusion(bf16[16384,512]{1,0:T(8,128)(2,1)} %param.5, bf16[128,4,16384]{2,1,0:T(4,128)(2,1)} %dot_general.5), kind=kOutput, calls=%fused_computation | convolution fusion | flops 8589934592 | bytes 34603008 | tf_op jit(solution)/shard_map/dot_general | solution.py:29
  271.1 0.7 copy.6
  271.8 24.7 %all_to_all.28 = f32[128,4,512]{2,1,0:T(4,128)S(1)} all-to-all(f32[128,4,512]{2,1,0:T(4,128)S(1)} %copy.6), channel_id=1, replica_groups=mesh['grp'=16,'tp'=8] {'grp','tp'}, dimensions={0} | all-to-all | bytes 2097152 | tf_op jit(solution)/shard_map/all_to_all | solution.py:36
  296.5 0.7 reduce_max.9
  297.1 0.7 fusion.4
  297.9 1.2 subtract_subtract_fusion
  (2 shorter events, 0.0 us)
